TPU v7x, 512 devices: a whole 4x4x16 slice. The times are simulated.
512 devices in a mesh: group: 2 (over core), ctx: 32 (over z, x_lo), tp: 8 (over y, x_hi).
Axes of the slice: x: 4 (x_hi: 2, x_lo: 2; x = x_hi * 2 + x_lo), y: 4, z: 16, core: 2. Of those that a mesh axis runs over, the one named last changes fastest.
Arguments:
- normed_hidden_rows: bfloat16 [8192, 8192], P(('group', 'ctx'), 'tp'), may hold values from -6 to 6
- queries: bfloat16 [8192, 8, 1024], P(('group', 'ctx'), 'tp'), may hold values from -500 to 500, as said below
- base_key_value: bfloat16 [8192, 8, 256], P(('group', 'ctx'), 'tp'), may hold values from -6 to 6
- row_adapter_index: int32 [8192], P(('group', 'ctx')), may hold values from 0 to 3
- adapter_down_weight: bfloat16 [8192, 512], P('tp'), may hold values from -0.0625 to 0.0625
- adapter_up_weight: bfloat16 [4, 2, 64, 8, 128], P(None, None, None, 'tp'), may hold values from -0.75 to 0.75
- key_value_cache: bfloat16 [1024, 128, 8, 256], P('ctx', None, 'tp'), may hold values from -6 to 6
- live_cache_length: int32 [1024], P('ctx'), may hold values from 1 to 128, as said below
- receiving_device: int32 [4096, 1], P('ctx'), may hold values from 0 to 31, as said below
- receiving_sequence: int32 [4096], P('ctx'), may hold values from 0 to 31, as said below
Outputs:
- attended: bfloat16 [8192, 8, 1024], P(('group', 'ctx'), 'tp')
Inputs may be any that keep to these rules, and one draw needn't show every extreme that they name: Large-magnitude queries occur. `live_cache_length`: lengths differ strongly from decode device to decode device; some sequence has exactly 128 live positions. `receiving_device`: prompt rows come in aligned pages of 8 consecutive rows; all rows of a page name one decode device, and the pages among the rows of one device name different decode devices. `receiving_sequence`: all rows of an aligned page of 8 consecutive rows name one sequence.
All inputs are finite; a program needn't handle non-finite values.
Results may differ from a plain program's by a relative error of at most 0.04.
Values may be sent and summed in bfloat16 or wider, within the bound.
A program may use at most 64 MiB of HBM per device.

v0:
```python
import math

import jax
import jax.numpy as jnp
from jax import lax
from jax.sharding import PartitionSpec as P


def shifted(value, axis, by):
    devices = lax.axis_size(axis)
    pairs = [(i, i + by) for i in range(devices) if 0 <= i + by < devices]
    return lax.ppermute(value, axis, pairs)


def bucket_rows(row_kv, dest_device, dest_slot, ctx_count, capacity):
    total_row_count = row_kv.shape[0]
    adapter_selector = (
        dest_device[:, None] == jnp.arange(ctx_count, dtype=jnp.int32)[None, :]
    ).astype(jnp.int32)
    position = jnp.sum((jnp.cumsum(adapter_selector, axis=0) - 1) * adapter_selector, axis=1)
    target = dest_device * capacity + position
    placing = target[None, :] == jnp.arange(ctx_count * capacity, dtype=jnp.int32)[:, None]
    outgoing = jnp.dot(
        placing.astype(jnp.bfloat16),
        row_kv.reshape(total_row_count, -1),
        preferred_element_type=jnp.float32,
    ).astype(jnp.bfloat16)
    seq_ids = jnp.sum(jnp.where(placing, dest_slot[None, :] + 1, 0), axis=1) - 1
    return (outgoing.reshape(ctx_count, capacity, -1), seq_ids.reshape(ctx_count, capacity))


def decode_block(queries, fresh, cache_rows, seq_lengths, handed, handed_seq):
    key_value_head_count = fresh.shape[1]
    head_extent = fresh.shape[2] // 2
    seq_count = seq_lengths.shape[0]
    step_count = fresh.shape[0] // seq_count
    per_head = queries.shape[2] // head_extent
    positions = cache_rows.shape[1]
    inv_root = 1.0 / math.sqrt(head_extent)
    grouped = queries.reshape(seq_count, step_count, key_value_head_count, per_head, head_extent)
    fresh_rows = fresh.reshape(seq_count, step_count, key_value_head_count, 2 * head_extent)
    cache_scores = jnp.einsum(
        "nkgqd,npgd->nkgqp",
        grouped,
        cache_rows[..., :head_extent],
        preferred_element_type=jnp.float32,
    )
    hand_scores = jnp.einsum(
        "nkgqd,mgd->nkgqm", grouped, handed[..., :head_extent], preferred_element_type=jnp.float32
    )
    fresh_scores = jnp.einsum(
        "nkgqd,njgd->nkgqj",
        grouped,
        fresh_rows[..., :head_extent],
        preferred_element_type=jnp.float32,
    )
    scores = jnp.concatenate([cache_scores, hand_scores, fresh_scores], axis=-1) * inv_root
    seq_index = jnp.arange(seq_count, dtype=jnp.int32)
    step_index = jnp.arange(step_count, dtype=jnp.int32)
    cache_ok = jnp.arange(positions, dtype=jnp.int32)[None, :] < seq_lengths[:, None]
    hand_ok = handed_seq[None, :] == seq_index[:, None]
    fresh_ok = step_index[None, :] <= step_index[:, None]
    lead = (seq_count, step_count, key_value_head_count, per_head)
    allowed = jnp.concatenate(
        [
            jnp.broadcast_to(cache_ok[:, None, None, None, :], lead + (positions,)),
            jnp.broadcast_to(hand_ok[:, None, None, None, :], lead + (handed.shape[0],)),
            jnp.broadcast_to(fresh_ok[None, :, None, None, :], lead + (step_count,)),
        ],
        axis=-1,
    )
    scores = jnp.where(allowed, scores, -1e30)
    peak = jnp.max(scores, axis=-1, keepdims=True)
    expos = jnp.where(allowed, jnp.exp(scores - peak), 0.0)
    weights = (expos / jnp.sum(expos, axis=-1, keepdims=True)).astype(jnp.bfloat16)
    split_hand = positions + handed.shape[0]
    result = jnp.einsum(
        "nkgqp,npgd->nkgqd",
        weights[..., :positions],
        cache_rows[..., head_extent:],
        preferred_element_type=jnp.float32,
    )
    result = result + jnp.einsum(
        "nkgqm,mgd->nkgqd",
        weights[..., positions:split_hand],
        handed[..., head_extent:],
        preferred_element_type=jnp.float32,
    )
    result = result + jnp.einsum(
        "nkgqj,njgd->nkgqd",
        weights[..., split_hand:],
        fresh_rows[..., head_extent:],
        preferred_element_type=jnp.float32,
    )
    return result.reshape(seq_count * step_count, key_value_head_count, per_head * head_extent)


def body(
    normed_hidden_rows,
    queries,
    base_key_value,
    row_adapter_index,
    adapter_down_weight,
    adapter_up_weight,
    key_value_cache,
    live_cache_length,
    receiving_device,
    receiving_sequence,
):
    total_row_count = normed_hidden_rows.shape[0]
    key_value_head_count = base_key_value.shape[1]
    head_extent = base_key_value.shape[2] // 2
    adapter_table = adapter_up_weight.shape[0]
    adapter_rank_size = adapter_up_weight.shape[2]
    per_head = queries.shape[2] // head_extent
    inv_root = 1.0 / math.sqrt(head_extent)
    value_partial = jnp.dot(
        normed_hidden_rows, adapter_down_weight, preferred_element_type=jnp.float32
    )
    adapter_selector = (
        row_adapter_index[:, None] == jnp.arange(adapter_table, dtype=jnp.int32)[None, :]
    )
    empty_value = jnp.zeros((), jnp.bfloat16)
    accumulated_sum = lax.psum(value_partial, "tp").astype(jnp.bfloat16)
    gathered_adapter = jnp.where(
        adapter_selector[:, :, None],
        accumulated_sum.reshape(total_row_count, adapter_table, 2 * adapter_rank_size),
        empty_value,
    )
    gathered_adapter = gathered_adapter.reshape(
        total_row_count, adapter_table, 2, adapter_rank_size
    )
    key_correction = jnp.dot(
        gathered_adapter[:, :, 0, :].reshape(total_row_count, adapter_table * adapter_rank_size),
        adapter_up_weight[:, 0].reshape(
            adapter_table * adapter_rank_size, key_value_head_count * head_extent
        ),
        preferred_element_type=jnp.float32,
    )
    value_correction = jnp.dot(
        gathered_adapter[:, :, 1, :].reshape(total_row_count, adapter_table * adapter_rank_size),
        adapter_up_weight[:, 1].reshape(
            adapter_table * adapter_rank_size, key_value_head_count * head_extent
        ),
        preferred_element_type=jnp.float32,
    )
    delta = jnp.concatenate(
        [
            key_correction.reshape(total_row_count, key_value_head_count, head_extent),
            value_correction.reshape(total_row_count, key_value_head_count, head_extent),
        ],
        axis=2,
    )
    projected_key_value = (base_key_value.astype(jnp.float32) + delta).astype(jnp.bfloat16)
    is_prefill = lax.axis_index("group") == 0
    row_start = lax.axis_index("ctx") * total_row_count
    grouped = queries.reshape(total_row_count, key_value_head_count, per_head, head_extent)
    query_pos = row_start + jnp.arange(total_row_count, dtype=jnp.int32)

    def add_keys(running, key_block, first_row):
        running_max, totals, weighted = running
        scores = (
            jnp.einsum(
                "tgqd,sgd->tgqs",
                grouped,
                key_block[:, :, :head_extent],
                preferred_element_type=jnp.float32,
            )
            * inv_root
        )
        key_pos = first_row + jnp.arange(key_block.shape[0], dtype=jnp.int32)
        allowed = (key_pos[None, :] <= query_pos[:, None])[:, None, None, :]
        scores = jnp.where(allowed, scores, -1e30)
        new_max = jnp.maximum(running_max, jnp.max(scores, axis=-1))
        expos = jnp.where(allowed, jnp.exp(scores - new_max[..., None]), 0.0)
        rescale = jnp.exp(running_max - new_max)
        totals = totals * rescale + jnp.sum(expos, axis=-1)
        weighted = weighted * rescale[..., None] + jnp.einsum(
            "tgqs,sgd->tgqd",
            expos.astype(jnp.bfloat16),
            key_block[:, :, head_extent:],
            preferred_element_type=jnp.float32,
        )
        return (new_max, totals, weighted)

    init_state = (
        jnp.full((total_row_count, key_value_head_count, per_head), -1e30, jnp.float32),
        jnp.zeros((total_row_count, key_value_head_count, per_head), jnp.float32),
        jnp.zeros((total_row_count, key_value_head_count, per_head, head_extent), jnp.float32),
    )
    key_piece = lax.all_gather(projected_key_value, "ctx", axis=0, tiled=True)
    piece_rows = key_piece.shape[0]
    key_span = math.gcd(piece_rows, 512)

    def one_span(span_index, inner_state):
        key_block = lax.dynamic_slice_in_dim(key_piece, span_index * key_span, key_span, 0)
        return add_keys(inner_state, key_block, span_index * key_span)

    def all_spans(inner_state):
        return lax.fori_loop(0, piece_rows // key_span, one_span, inner_state)

    def unchanged(inner_state):
        return inner_state

    active = jnp.logical_and(is_prefill, jnp.int32(0) <= row_start + total_row_count - 1)
    running_max, totals, weighted = lax.cond(active, all_spans, unchanged, init_state)
    ctx_count = lax.axis_size("ctx")
    capacity = max(2, 2 * total_row_count // ctx_count)
    dest_device = receiving_device.reshape(-1)
    outgoing, seq_ids = bucket_rows(
        projected_key_value, dest_device, receiving_sequence, ctx_count, capacity
    )
    landed_rows, landed_ids = (
        lax.all_to_all(outgoing, "ctx", split_axis=0, concat_axis=0, tiled=True),
        lax.all_to_all(seq_ids, "ctx", split_axis=0, concat_axis=0, tiled=True),
    )
    received, handed_seq = shifted((landed_rows, landed_ids), "group", 1)
    handed = received.reshape(ctx_count * capacity, key_value_head_count, 2 * head_extent)
    handed_seq = handed_seq.reshape(-1)

    def prompt_result():
        return (weighted / totals[..., None]).reshape(
            total_row_count, key_value_head_count, per_head * head_extent
        )

    def decode_result():
        return decode_block(
            queries, projected_key_value, key_value_cache, live_cache_length, handed, handed_seq
        )

    return lax.cond(is_prefill, prompt_result, decode_result).astype(jnp.bfloat16)


def solution(mesh):
    return jax.shard_map(
        body,
        mesh=mesh,
        in_specs=(
            P(("group", "ctx"), "tp"),
            P(("group", "ctx"), "tp", None),
            P(("group", "ctx"), "tp", None),
            P(("group", "ctx")),
            P("tp", None),
            P(None, None, None, "tp", None),
            P("ctx", None, "tp", None),
            P("ctx"),
            P("ctx", None),
            P("ctx"),
        ),
        out_specs=P(("group", "ctx"), "tp", None),
        check_vma=False,
    )
```

profile of v0, /device:TPU:2, one launch (start us, length us, event | category | flops | bytes accessed | tf_op | source)
XLA Modules:
  0.0 257.0 jit_solution(6768413359709735340)
XLA Ops:
  6.6 1.1 copy-done
  7.8 1.3 fusion.36
  9.0 45.5 %all-reduce.1 = bf16[128,512]{1,0:T(8,128)(2,1)S(1)} all-reduce(f32[128,512]{1,0:T(8,128)S(1)} %fusion.36), channel_id=1, replica_groups=mesh['group'=2,'ctx'=32,'tp'=8] {'tp'}, use_global_device_ids=true, to_apply=%region_0.0 | all-reduce | flops 65536 | bytes 393216 | tf_op jit(solution)/shard_map/psum | solution.py:124
  56.4 1.7 fusion.29
  58.1 17.0 %all-to-all-start.1 = ((bf16[32,8,256]{2,1,0:T(8,128)(2,1)}), bf16[32,8,256]{2,1,0:T(8,128)(2,1)S(1)}, u32[]{:S(2)}, u32[]{:S(2)}) async-start(bf16[32,8,256]{2,1,0:T(8,128)(2,1)} %fusion.29), calls=%async_computation.1 | async-start | bytes 262144 | tf_op jit(solution)/shard_map/all_to_all | solution.py:214
  75.3 15.3 %all-to-all-done.1 = bf16[32,8,256]{2,1,0:T(8,128)(2,1)S(1)} async-done(((bf16[32,8,256]{2,1,0:T(8,128)(2,1)}), bf16[32,8,256]{2,1,0:T(8,128)(2,1)S(1)}, u32[]{:S(2)}, u32[]{:S(2)}) %all-to-all-start.1) | async-done | bytes 131104 | tf_op jit(solution)/shard_map/all_to_all | solution.py:214
  90.6 1.3 collective-permute-start.1
  92.6 3.6 %all-to-all-start = ((s32[32,1,8]{2,1,0:T(1,128)}), s32[32,1,8]{2,1,0:T(1,128)S(1)}, u32[]{:S(2)}, u32[]{:S(2)}) async-start(s32[32,1,8]{2,1,0:T(1,128)} %bitcast.40), calls=%async_computation | async-start | bytes 32768 | tf_op jit(solution)/shard_map/all_to_all | solution.py:215
  96.2 12.1 %all-to-all-done = s32[32,1,8]{2,1,0:T(1,128)S(1)} async-done(((s32[32,1,8]{2,1,0:T(1,128)}), s32[32,1,8]{2,1,0:T(1,128)S(1)}, u32[]{:S(2)}, u32[]{:S(2)}) %all-to-all-start) | async-done | bytes 1056 | tf_op jit(solution)/shard_map/all_to_all | solution.py:215
  108.3 1.3 collective-permute-start
  110.5 84.1 %all-gather.2.cloned.1.call-done = bf16[4096,1,256]{0,2,1:T(8,128)(2,1)} async-done(((bf16[128,1,256]{0,2,1:T(8,128)(2,1)}), bf16[4096,1,256]{0,2,1:T(8,128)(2,1)}) %all-gather.2.cloned.1.call-update) | async-done | bytes 2097168 | tf_op jit(solution)/shard_map/all_gather | solution.py:191
  194.6 0.8 copy-done.3
  195.4 51.6 %conditional.7 = (f32[128,1,8]{0,2,1:T(8,128)}, f32[128,1,8,128]{0,3,2,1:T(8,128)}) conditional(s32[]{:T(128)} %convert_element_type.63, () %tuple.43, (s32[128]{0:T(128)}, bf16[4096,1,256]{0,2,1:T(8,128)(2,1)}, bf16[128,1,8,128]{0,3,2,1:T(8,128)(2,1)S(1)}) %tuple.87), branch_computations={%region_4.0_spmd, %region_5.10_spmd} | conditional | flops 275716608 | bytes 8721219 | solution.py:206
  195.6 51.4 %while.17 = (s32[]{:T(128)}, f32[128,1,8]{0,2,1:T(8,128)S(1)}, f32[128,1,8]{0,2,1:T(8,128)}, f32[128,1,8,128]{0,3,2,1:T(8,128)}, s32[128]{0:T(128)}, /*index=5*/...) while((s32[]{:T(128)}, f32[128,1,8]{0,2,1:T(8,128)S(1)}, ...), condition=%wide.region_9.9_spmd.clone, body=%wide.region_6.0_spmd.clone.sunk | while | flops 275716608 | bytes 8196811 | solution.py:200
  195.7 0.7 broadcast_compare_fusion.2
  196.4 1.4 fusion.51
  197.8 2.4 fusion.54
  201.3 0.7 broadcast_compare_fusion.2
  202.0 1.4 fusion.51
  203.4 2.6 %fusion.54 = f32[128,1,8,128]{0,3,2,1:T(8,128)} fusion(f32[512,128,8]{1,0,2:T(8,128)S(1)} %get-tuple-element.318, f32[128,8]{0,1:T(8,128)S(1)} %bitcast.200, pred[128,512]{0,1:T(8,128)(4,1)S(1)} %broadcast_compare_fusion.2, f32[128,1,8,128]{0,3,2,1:T(8,128)} %get-tuple-element.335, f32[128,8]{0,1:T(8,128)S(1)} %get-tuple-element.319, ...), kind=kOutput, calls=%fused_computation.38.clone.1 | convolution fusion | flops 137232384 | bytes 3350537 | tf_op jit(solution)/shard_map/cond/branch_1_fun/while/body/eval_jaxpr/tgqs,sgd->tgqd/dot_general | solution.py:178
  206.6 1.3 bitcast_add_fusion.2
  207.9 0.7 broadcast_compare_fusion.2
  208.6 1.4 fusion.51
  210.0 2.6 %fusion.54 = f32[128,1,8,128]{0,3,2,1:T(8,128)} fusion(f32[512,128,8]{1,0,2:T(8,128)S(1)} %get-tuple-element.318, f32[128,8]{0,1:T(8,128)S(1)} %bitcast.200, pred[128,512]{0,1:T(8,128)(4,1)S(1)} %broadcast_compare_fusion.2, f32[128,1,8,128]{0,3,2,1:T(8,128)} %get-tuple-element.335, f32[128,8]{0,1:T(8,128)S(1)} %get-tuple-element.319, ...), kind=kOutput, calls=%fused_computation.38.clone.1 | convolution fusion | flops 137232384 | bytes 3350537 | tf_op jit(solution)/shard_map/cond/branch_1_fun/while/body/eval_jaxpr/tgqs,sgd->tgqd/dot_general | solution.py:178
  213.1 1.3 bitcast_add_fusion.2
  214.4 0.7 broadcast_compare_fusion.2
  215.1 1.4 fusion.51
  216.5 2.6 %fusion.54 = f32[128,1,8,128]{0,3,2,1:T(8,128)} fusion(f32[512,128,8]{1,0,2:T(8,128)S(1)} %get-tuple-element.318, f32[128,8]{0,1:T(8,128)S(1)} %bitcast.200, pred[128,512]{0,1:T(8,128)(4,1)S(1)} %broadcast_compare_fusion.2, f32[128,1,8,128]{0,3,2,1:T(8,128)} %get-tuple-element.335, f32[128,8]{0,1:T(8,128)S(1)} %get-tuple-element.319, ...), kind=kOutput, calls=%fused_computation.38.clone.1 | convolution fusion | flops 137232384 | bytes 3350537 | tf_op jit(solution)/shard_map/cond/branch_1_fun/while/body/eval_jaxpr/tgqs,sgd->tgqd/dot_general | solution.py:178
  219.6 1.3 bitcast_add_fusion.2
  220.9 0.7 broadcast_compare_fusion.2
  221.6 1.4 fusion.51
  223.0 2.6 %fusion.54 = f32[128,1,8,128]{0,3,2,1:T(8,128)} fusion(f32[512,128,8]{1,0,2:T(8,128)S(1)} %get-tuple-element.318, f32[128,8]{0,1:T(8,128)S(1)} %bitcast.200, pred[128,512]{0,1:T(8,128)(4,1)S(1)} %broadcast_compare_fusion.2, f32[128,1,8,128]{0,3,2,1:T(8,128)} %get-tuple-element.335, f32[128,8]{0,1:T(8,128)S(1)} %get-tuple-element.319, ...), kind=kOutput, calls=%fused_computation.38.clone.1 | convolution fusion | flops 137232384 | bytes 3350537 | tf_op jit(solution)/shard_map/cond/branch_1_fun/while/body/eval_jaxpr/tgqs,sgd->tgqd/dot_general | solution.py:178
  226.2 1.3 bitcast_add_fusion.2
  227.4 0.7 broadcast_compare_fusion.2
  228.2 1.4 fusion.51
  229.6 2.6 %fusion.54 = f32[128,1,8,128]{0,3,2,1:T(8,128)} fusion(f32[512,128,8]{1,0,2:T(8,128)S(1)} %get-tuple-element.318, f32[128,8]{0,1:T(8,128)S(1)} %bitcast.200, pred[128,512]{0,1:T(8,128)(4,1)S(1)} %broadcast_compare_fusion.2, f32[128,1,8,128]{0,3,2,1:T(8,128)} %get-tuple-element.335, f32[128,8]{0,1:T(8,128)S(1)} %get-tuple-element.319, ...), kind=kOutput, calls=%fused_computation.38.clone.1 | convolution fusion | flops 137232384 | bytes 3350537 | tf_op jit(solution)/shard_map/cond/branch_1_fun/while/body/eval_jaxpr/tgqs,sgd->tgqd/dot_general | solution.py:178
  232.7 1.3 bitcast_add_fusion.2
  234.0 0.7 broadcast_compare_fusion.2
  234.7 1.4 fusion.51
  236.1 2.6 %fusion.54 = f32[128,1,8,128]{0,3,2,1:T(8,128)} fusion(f32[512,128,8]{1,0,2:T(8,128)S(1)} %get-tuple-element.318, f32[128,8]{0,1:T(8,128)S(1)} %bitcast.200, pred[128,512]{0,1:T(8,128)(4,1)S(1)} %broadcast_compare_fusion.2, f32[128,1,8,128]{0,3,2,1:T(8,128)} %get-tuple-element.335, f32[128,8]{0,1:T(8,128)S(1)} %get-tuple-element.319, ...), kind=kOutput, calls=%fused_computation.38.clone.1 | convolution fusion | flops 137232384 | bytes 3350537 | tf_op jit(solution)/shard_map/cond/branch_1_fun/while/body/eval_jaxpr/tgqs,sgd->tgqd/dot_general | solution.py:178
  239.2 1.3 bitcast_add_fusion.2
  240.5 0.7 broadcast_compare_fusion.2
  241.2 1.4 fusion.51
  242.6 2.6 %fusion.54 = f32[128,1,8,128]{0,3,2,1:T(8,128)} fusion(f32[512,128,8]{1,0,2:T(8,128)S(1)} %get-tuple-element.318, f32[128,8]{0,1:T(8,128)S(1)} %bitcast.200, pred[128,512]{0,1:T(8,128)(4,1)S(1)} %broadcast_compare_fusion.2, f32[128,1,8,128]{0,3,2,1:T(8,128)} %get-tuple-element.335, f32[128,8]{0,1:T(8,128)S(1)} %get-tuple-element.319, ...), kind=kOutput, calls=%fused_computation.38.clone.1 | convolution fusion | flops 137232384 | bytes 3350537 | tf_op jit(solution)/shard_map/cond/branch_1_fun/while/body/eval_jaxpr/tgqs,sgd->tgqd/dot_general | solution.py:178
  245.7 1.3 bitcast_add_fusion.2
  247.0 2.4 conditional.8
  247.0 1.3 copy.79
  248.3 0.8 copy.68
  (81 shorter events, 9.5 us)
Async XLA Ops:
  6.5 1.2 copy-start
  6.5 48.1 %copy-start.14 = (s32[128]{0:T(128)S(1)}, s32[128]{0:T(128)}, u32[]{:S(2)}) copy-start(s32[128]{0:T(128)} %param.19) | copy-start | bytes 1540
  6.5 48.2 %copy-start.5 = (bf16[4,2,64,1,128]{4,2,3,1,0:T(8,128)(2,1)S(1)}, bf16[4,2,64,1,128]{4,2,3,1,0:T(8,128)(2,1)}, u32[]{:S(2)}) copy-start(bf16[4,2,64,1,128]{4,2,3,1,0:T(8,128)(2,1)} %param.21) | copy-start | bytes 393220
  6.5 48.2 %copy-start.8 = (bf16[128,1,256]{2,0,1:T(8,128)(2,1)S(1)}, bf16[128,1,256]{2,0,1:T(8,128)(2,1)}, u32[]{:S(2)}) copy-start(bf16[128,1,256]{2,0,1:T(8,128)(2,1)} %param.18) | copy-start | bytes 196612
  6.5 49.4 %copy-start.11 = (s32[128,1]{0,1:T(1,128)S(1)}, s32[128,1]{0,1:T(1,128)}, u32[]{:S(2)}) copy-start(s32[128,1]{0,1:T(1,128)} %param.24) | copy-start | bytes 1540
  6.5 49.9 %copy-start.12 = (s32[128]{0:T(128)S(1)}, s32[128]{0:T(128)}, u32[]{:S(2)}) copy-start(s32[128]{0:T(128)} %param.25) | copy-start | bytes 1540
  6.6 103.6 %copy-start.2 = (bf16[128,1,1024]{2,0,1:T(8,128)(2,1)S(1)}, bf16[128,1,1024]{2,0,1:T(8,128)(2,1)}, u32[]{:S(2)}) copy-start(bf16[128,1,1024]{2,0,1:T(8,128)(2,1)} %param.17) | copy-start | bytes 786436
  6.6 188.0 %all-gather.2.cloned.1.call-start = ((), (), s32[]{:S(2)}) async-start(), calls=%async_computation.2 | async-start | bytes 2162688 | tf_op jit(solution)/shard_map/all_gather | solution.py:191
  58.1 32.5 %all-to-all-start.1 = ((bf16[32,8,256]{2,1,0:T(8,128)(2,1)}), bf16[32,8,256]{2,1,0:T(8,128)(2,1)S(1)}, u32[]{:S(2)}, u32[]{:S(2)}) async-start(bf16[32,8,256]{2,1,0:T(8,128)(2,1)} %fusion.29), calls=%async_computation.1 | async-start | bytes 262144 | tf_op jit(solution)/shard_map/all_to_all | solution.py:214
  90.6 19.9 %collective-permute-start.1 = (bf16[32,8,256]{2,1,0:T(8,128)(2,1)S(1)}, bf16[32,8,256]{2,1,0:T(8,128)(2,1)S(1)}, u32[]{:S(2)}, u32[]{:S(2)}) collective-permute-start(bf16[32,8,256]{2,1,0:T(8,128)(2,1)S(1)} %all-to-all-done.1), channel_id=1, source_target_pairs={{0,256},{1,257},{2,258},{3,259},{4,260},{5,261},{6,262},{7,263},{8... | collective-permute-start | bytes 393224 | tf_op jit(solution)/shard_map/ppermute | solution.py:12
  92.6 15.7 %all-to-all-start = ((s32[32,1,8]{2,1,0:T(1,128)}), s32[32,1,8]{2,1,0:T(1,128)S(1)}, u32[]{:S(2)}, u32[]{:S(2)}) async-start(s32[32,1,8]{2,1,0:T(1,128)} %bitcast.40), calls=%async_computation | async-start | bytes 32768 | tf_op jit(solution)/shard_map/all_to_all | solution.py:215
  108.3 2.1 collective-permute-start
  110.5 84.2 %copy-start.9 = (s32[32,8]{1,0:T(8,128)}, s32[32,8]{1,0:T(8,128)S(1)}, u32[]{:S(2)}) copy-start(s32[32,8]{1,0:T(8,128)S(1)} %collective-permute-done) | copy-start | bytes 3076
  110.5 84.2 %copy-start.6 = (bf16[32,8,256]{2,1,0:T(8,128)(2,1)}, bf16[32,8,256]{2,1,0:T(8,128)(2,1)S(1)}, u32[]{:S(2)}) copy-start(bf16[32,8,256]{2,1,0:T(8,128)(2,1)S(1)} %collective-permute-done.1) | copy-start | bytes 393220
  194.6 0.8 copy-start.3
  249.4 0.7 copy-start.4
Sparse Core Ops, SparseCore 0:
  56.1 138.4 all-gather.1
where the time goes:
time: 258 us; the launch traced here: 257 us
  waiting for transfers between devices  112 us (43%)
  blocking collectives  45.5 us (18%)
  matrix products  35 us (14%)
  starting transfers between devices  23.2 us (9%)
  other arithmetic  21.4 us (8%)
  between operations  13.6 us (5%)
  local copies, waits for them, and re-layouts  6.18 us (2%)
    all_gather x1, waiting for transfers between devices, body(): key_piece = lax.all_gather(projected_key_value, 'ctx', axis=0, tiled=True)  84.1 us
    psum x1, blocking collectives, body(): accumulated_sum = lax.psum(value_partial, 'tp').astype(jnp.bfloat16)  45.5 us
    dot_general x8, matrix products, add_keys(): jnp.einsum('tgqs,sgd->tgqd', expos.astype(jnp.bfloat16), key_block[:, :,...  20.5 us
    all_to_all x1, starting transfers between devices, body(): lax.all_to_all(outgoing, 'ctx', split_axis=0, concat_axis=0, tiled=True)  17 us
    all_to_all x1, waiting for transfers between devices, body(): lax.all_to_all(outgoing, 'ctx', split_axis=0, concat_axis=0, tiled=True)  15.3 us
    all_to_all x1, waiting for transfers between devices, body(): lax.all_to_all(seq_ids, 'ctx', split_axis=0, concat_axis=0, tiled=True)  12.1 us
    dot_general x8, matrix products, add_keys(): jnp.einsum('tgqd,sgd->tgqs', grouped, key_block[:, :, :head_extent], pref...  11.1 us
    add x8, other arithmetic, add_keys(): totals = totals * rescale + jnp.sum(expos, axis=-1)  9.66 us
  transfers between devices with their start and end apart: 5, of which 4 were waited for; matrix products, arithmetic and copies ran while one was open for 1% of the time, Pallas kernels for 0%

commit v1 on v0

v1 whole, which is shorter than its diff:
```python
import math

import jax
import jax.numpy as jnp
from jax import lax
from jax.experimental import pallas as pl
from jax.experimental.pallas import tpu as pltpu
from jax.sharding import PartitionSpec as P

MESH = pl.DeviceIdType.MESH
ROWS = 128
HEADS = 8
HEAD = 128
RANK2 = 128
ADAPTERS = 4
SEQ_DEV = 32
CACHE = 128
IDROWS = 16
BLOCK = ROWS + IDROWS
NZ = 16
NTP = 8
QROWS = ROWS * HEADS
GROUPS = 8
NEG = -1e30
SCALE = math.log2(math.e) / math.sqrt(HEAD)

OWN_SENDS = [(0, 4, 4), (0, -4, 12), (0, 2, 2), (0, -2, 14), (0, 1, 1), (0, -1, 15)]
FORWARDS = {
    4: [(4, 4, 8), (4, 2, 6), (4, 1, 5)],
    12: [(12, -2, 10), (12, -1, 11)],
    2: [(2, 1, 3)],
    14: [(14, -1, 13)],
    6: [(6, 1, 7)],
    10: [(10, -1, 9)],
}
ALL_SENDS = OWN_SENDS + [s for v in FORWARDS.values() for s in v]
Z_SEM = {send[2]: i for i, send in enumerate(ALL_SENDS)}
X_SEM0 = len(ALL_SENDS)
CORE_SEM0 = X_SEM0 + NZ
SEND_SEMS = CORE_SEM0 + 2 * NZ

PROMPT_PLAN = [
    ("own", 1), ("own", 15), ("own", 2), ("own", 14), ("pair", 0),
    ("own", 4), ("own", 12), ("own", 3), ("own", 13),
    ("pair", 1), ("pair", 15), ("own", 5), ("own", 11), ("pair", 2), ("pair", 14),
    ("own", 6), ("own", 10), ("pair", 4), ("pair", 12),
    ("own", 8), ("pair", 3), ("pair", 13), ("own", 7), ("own", 9),
    ("pair", 5), ("pair", 11), ("pair", 6), ("pair", 10), ("pair", 8), ("pair", 7), ("pair", 9),
]
DECODE_PLAN = [0, 1, 15, 2, 14, 4, 12, 3, 13, 5, 11, 6, 10, 8, 7, 9]


def kernel(
    hid_ref, q_ref, base_ref, idx_ref, down_ref, up_ref, cache_ref, len_ref, rd_ref, rs_ref,
    out_ref,
    hid, qin, base, idx, down, up, cache, lens, rd, rs,
    part, landed, kv, fresh, q, top, acc, tot, wide,
    load_sem, tp_send, tp_recv, kv_send, kv_recv,
):
    group = lax.axis_index("group")
    ctx = lax.axis_index("ctx")
    tp = lax.axis_index("tp")
    z = ctx // 2
    x_lo = ctx % 2

    def z_peer(step):
        return {"ctx": lax.rem(z + step + NZ, NZ) * 2 + x_lo}

    x_peer = {"ctx": z * 2 + (1 - x_lo)}
    core_peer = {"group": 1 - group}

    barrier = pltpu.get_barrier_semaphore()
    peers = [{"tp": lax.rem(tp + d, NTP)} for d in range(1, NTP)]
    peers += [z_peer(s) for s in (4, -4, 2, -2, 1, -1)]
    peers += [x_peer, core_peer]
    for peer in peers:
        pl.semaphore_signal(barrier, inc=1, device_id=peer, device_id_type=MESH)

    loads = [
        pltpu.make_async_copy(src, dst, load_sem.at[i])
        for i, (src, dst) in enumerate(
            [(hid_ref, hid), (down_ref, down), (idx_ref, idx), (up_ref, up), (base_ref, base),
             (rd_ref, rd), (rs_ref, rs), (q_ref, qin), (len_ref, lens), (cache_ref, cache)]
        )
    ]
    for load in loads[:9]:
        load.start()

    @pl.when(group == 1)
    def _():
        loads[9].start()

    for load in loads[:3]:
        load.wait()

    eye = lax.broadcasted_iota(jnp.int32, (ROWS, ROWS), 0) == lax.broadcasted_iota(
        jnp.int32, (ROWS, ROWS), 1
    )
    adapter = jnp.sum(
        jnp.where(eye, jnp.broadcast_to(idx[...].astype(jnp.float32), (ROWS, ROWS)), 0.0),
        axis=1,
        keepdims=True,
    )
    shrunk = jnp.dot(hid[...], down[...], preferred_element_type=jnp.float32)
    picked = jnp.zeros((ROWS, RANK2), jnp.float32)
    for a in range(ADAPTERS):
        picked = jnp.where(adapter == float(a), shrunk[:, a * RANK2 : (a + 1) * RANK2], picked)
    part[...] = picked
    pl.semaphore_wait(barrier, len(peers))

    tp_copies = [
        pltpu.make_async_remote_copy(
            src_ref=part,
            dst_ref=landed.at[d],
            send_sem=tp_send.at[d],
            recv_sem=tp_recv.at[d],
            device_id={"tp": lax.rem(tp + d, NTP)},
            device_id_type=MESH,
        )
        for d in range(1, NTP)
    ]
    for d in (3, 5, 4, 7, 1, 6, 2):
        tp_copies[d - 1].start()

    for load in loads[3:9]:
        load.wait()
    for g in range(GROUPS):
        for j in range(HEADS):
            q[g * 128 + j * 16 : g * 128 + (j + 1) * 16, :] = qin[
                g * 16 : (g + 1) * 16, j * HEAD : (j + 1) * HEAD
            ]
    is_key = (lax.broadcasted_iota(jnp.int32, (ADAPTERS * RANK2, HEAD), 0) // 64) % 2 == 0
    zero = jnp.zeros((), jnp.float32)
    up_f = up[...].astype(jnp.float32)
    wide[:, :HEAD] = jnp.where(is_key, up_f, zero).astype(jnp.bfloat16)
    wide[:, HEAD:] = jnp.where(is_key, zero, up_f).astype(jnp.bfloat16)

    def scores_of(queries, keys):
        return lax.dot_general(
            queries, keys, (((1,), (1,)), ((), ())), preferred_element_type=jnp.float32
        )

    def weighted(weights, values):
        ones = jnp.ones(values.shape, jnp.bfloat16)
        return jnp.dot(
            weights.astype(jnp.bfloat16),
            jnp.concatenate([values, ones], axis=1),
            preferred_element_type=jnp.float32,
        )

    def first_keys(rows, scores, values):
        peak = jnp.max(scores, axis=1, keepdims=True)
        both = weighted(jnp.exp2((scores - peak) * SCALE), values)
        top[rows, :] = jnp.broadcast_to(peak, (peak.shape[0], HEAD))
        acc[rows, :] = both[:, :HEAD]
        tot[rows, :] = both[:, HEAD:]

    def more_keys(rows, scores, values):
        before = top[rows, :]
        after = jnp.maximum(before, jnp.max(scores, axis=1, keepdims=True))
        rescale = jnp.exp2((before - after) * SCALE)
        both = weighted(jnp.exp2((scores - after[:, :1]) * SCALE), values)
        top[rows, :] = after
        acc[rows, :] = acc[rows, :] * rescale + both[:, :HEAD]
        tot[rows, :] = tot[rows, :] * rescale + both[:, HEAD:]

    def row_token(first, count):
        row = lax.broadcasted_iota(jnp.int32, (count, 1), 0) + first
        return (row // 128) * 16 + row % 16

    STEP = 256

    def by_rows(body):
        def one(i, carry):
            first = pl.multiple_of(i * STEP, STEP)
            body(pl.ds(first, STEP), first)
            return carry

        lax.fori_loop(0, QROWS // STEP, one, 0)

    @pl.when(group == 1)
    def _():
        loads[9].wait()
        column = lax.broadcasted_iota(jnp.int32, (1, CACHE), 1)
        for g in range(GROUPS):
            rows = pl.ds(g * 128, 128)
            block = cache[4 * g : 4 * g + 4].reshape(4 * CACHE, 2 * HEAD)
            scores = scores_of(q[rows, :], block[:, :HEAD])
            own = (lax.broadcasted_iota(jnp.int32, (128, 1), 0) % 16) // 4
            pieces = []
            for n in range(4):
                ok = jnp.logical_and(own == n, column < lens[4 * g + n])
                pieces.append(jnp.where(ok, scores[:, n * CACHE : (n + 1) * CACHE], NEG))
            first_keys(rows, jnp.concatenate(pieces, axis=1), block[:, HEAD:])

    for copy in tp_copies:
        copy.wait_recv()
    total = picked
    for d in range(1, NTP):
        total = total + landed[d]
    spread = jnp.concatenate(
        [
            jnp.where(adapter == float(a), total, 0.0).astype(jnp.bfloat16)
            for a in range(ADAPTERS)
        ],
        axis=1,
    )
    delta = jnp.dot(spread, wide[...], preferred_element_type=jnp.float32)
    own_kv = (base[...].astype(jnp.float32) + delta).astype(jnp.bfloat16)

    def z_copy(source, step, dest):
        i = Z_SEM[dest]
        return pltpu.make_async_remote_copy(
            src_ref=kv.at[source, 0], dst_ref=kv.at[dest, 0],
            send_sem=kv_send.at[i], recv_sem=kv_recv.at[2 * dest],
            device_id=z_peer(step), device_id_type=MESH,
        )

    def x_copy(slot):
        return pltpu.make_async_remote_copy(
            src_ref=kv.at[slot, 0], dst_ref=kv.at[slot, 1],
            send_sem=kv_send.at[X_SEM0 + slot], recv_sem=kv_recv.at[2 * slot + 1],
            device_id=x_peer, device_id_type=MESH,
        )

    def core_copy(slot, side):
        return pltpu.make_async_remote_copy(
            src_ref=kv.at[slot, side], dst_ref=kv.at[slot, side],
            send_sem=kv_send.at[CORE_SEM0 + 2 * slot + side],
            recv_sem=kv_recv.at[2 * slot + side],
            device_id=core_peer, device_id_type=MESH,
        )

    def pair_of(slot):
        keys = jnp.concatenate([kv[slot, 0, :ROWS, :HEAD], kv[slot, 1, :ROWS, :HEAD]], axis=0)
        values = jnp.concatenate([kv[slot, 0, :ROWS, HEAD:], kv[slot, 1, :ROWS, HEAD:]], axis=0)
        return keys, values

    @pl.when(group == 0)
    def _():
        kv[0, 0, :ROWS, :] = own_kv
        ids = jnp.concatenate([rd[...], rs[...]], axis=1).astype(jnp.float32)
        kv[0, 0, ROWS:, :] = jnp.broadcast_to(ids, (IDROWS, 2 * HEAD)).astype(jnp.bfloat16)
        for send in OWN_SENDS:
            z_copy(*send).start()
        x_copy(0).start()
        core_copy(0, 0).start()

        def diagonal(rows, first):
            token = row_token(first, STEP)
            ok = lax.broadcasted_iota(jnp.int32, (1, ROWS), 1) <= token
            scores = jnp.where(ok, scores_of(q[rows, :], kv[0, 0, :ROWS, :HEAD]), NEG)
            first_keys(rows, scores, kv[0, 0, :ROWS, HEAD:])

        by_rows(diagonal)
        for what, slot in PROMPT_PLAN:
            if what == "own":
                z_copy(0, 1, slot).wait_recv()
                for send in FORWARDS.get(slot, []):
                    z_copy(*send).start()
                x_copy(slot).start()
                core_copy(slot, 0).start()
            else:
                x_copy(slot).wait_recv()
                core_copy(slot, 1).start()
                if slot == 0:

                    @pl.when(x_lo == 1)
                    def _():
                        def side(rows, first):
                            more_keys(
                                rows,
                                scores_of(q[rows, :], kv[0, 1, :ROWS, :HEAD]),
                                kv[0, 1, :ROWS, HEAD:],
                            )

                        by_rows(side)
                else:

                    @pl.when(z >= slot)
                    def _():
                        keys, values = pair_of(slot)

                        def both(rows, first):
                            more_keys(rows, scores_of(q[rows, :], keys), values)

                        by_rows(both)

    @pl.when(group == 1)
    def _():
        fresh[...] = own_kv
        me = ctx.astype(jnp.float32)

        def steps(rows, first):
            token = row_token(first, STEP)
            column = lax.broadcasted_iota(jnp.int32, (1, ROWS), 1)
            ok = jnp.logical_and(column // 4 == token // 4, column <= token)
            scores = jnp.where(ok, scores_of(q[rows, :], fresh[:, :HEAD]), NEG)
            more_keys(rows, scores, fresh[:, HEAD:])

        by_rows(steps)
        for slot in DECODE_PLAN:
            for side in (0, 1):
                core_copy(slot, side).wait_recv()
            keys, values = pair_of(slot)
            ids = jnp.concatenate(
                [kv[slot, 0, ROWS:, :], kv[slot, 1, ROWS:, :]], axis=0
            ).astype(jnp.float32)
            device = jnp.concatenate([ids[:1, :HEAD], ids[IDROWS : IDROWS + 1, :HEAD]], axis=1)
            sequence = jnp.concatenate([ids[:1, HEAD:], ids[IDROWS : IDROWS + 1, HEAD:]], axis=1)
            code = jnp.where(device == me, sequence, -1.0)

            def handed(rows, first):
                own = (row_token(first, STEP) // 4).astype(jnp.float32)
                scores = jnp.where(code == own, scores_of(q[rows, :], keys), NEG)
                more_keys(rows, scores, values)

            by_rows(handed)

    for g in range(GROUPS):
        rows = pl.ds(g * 128, 128)
        result = (acc[rows, :] / tot[rows, :]).astype(jnp.bfloat16)
        for j in range(HEADS):
            out_ref[g * 16 : (g + 1) * 16, j * HEAD : (j + 1) * HEAD] = result[
                j * 16 : (j + 1) * 16
            ]

    for copy in tp_copies:
        copy.wait_send()

    @pl.when(group == 0)
    def _():
        for send in ALL_SENDS:
            z_copy(*send).wait_send()
        for slot in range(NZ):
            x_copy(slot).wait_send()
            core_copy(slot, 0).wait_send()
            core_copy(slot, 1).wait_send()


def body(hidden, queries, base, adapter, down, up, cache, lengths, device, sequence):
    vmem = pltpu.VMEM
    bf16, f32, i32 = jnp.bfloat16, jnp.float32, jnp.int32
    out = pl.pallas_call(
        kernel,
        out_shape=jax.ShapeDtypeStruct((ROWS, HEADS * HEAD), bf16),
        in_specs=[pl.BlockSpec(memory_space=pl.ANY)] * 10,
        out_specs=pl.BlockSpec(memory_space=vmem),
        scratch_shapes=[
            vmem((ROWS, 1024), bf16),
            vmem((ROWS, HEADS * HEAD), bf16),
            vmem((ROWS, 2 * HEAD), bf16),
            vmem((1, ROWS), i32),
            vmem((1024, ADAPTERS * RANK2), bf16),
            vmem((ADAPTERS * RANK2, HEAD), bf16),
            vmem((SEQ_DEV, CACHE, 2 * HEAD), bf16),
            pltpu.SMEM((SEQ_DEV,), i32),
            vmem((1, ROWS), i32),
            vmem((1, ROWS), i32),
            vmem((ROWS, RANK2), f32),
            vmem((NTP, ROWS, RANK2), f32),
            vmem((NZ, 2, BLOCK, 2 * HEAD), bf16),
            vmem((ROWS, 2 * HEAD), bf16),
            vmem((QROWS, HEAD), bf16),
            vmem((QROWS, HEAD), f32),
            vmem((QROWS, HEAD), f32),
            vmem((QROWS, HEAD), f32),
            vmem((ADAPTERS * RANK2, 2 * HEAD), bf16),
            pltpu.SemaphoreType.DMA((10,)),
            pltpu.SemaphoreType.DMA((NTP,)),
            pltpu.SemaphoreType.DMA((NTP,)),
            pltpu.SemaphoreType.DMA((SEND_SEMS,)),
            pltpu.SemaphoreType.DMA((2 * NZ,)),
        ],
        compiler_params=pltpu.CompilerParams(
            collective_id=0, has_side_effects=True, vmem_limit_bytes=60 << 20
        ),
        name="attention",
    )(
        hidden,
        queries.reshape(ROWS, HEADS * HEAD),
        base.reshape(ROWS, 2 * HEAD),
        adapter.reshape(1, ROWS),
        down,
        up.reshape(ADAPTERS * RANK2, HEAD),
        cache.reshape(SEQ_DEV, CACHE, 2 * HEAD),
        lengths,
        device.reshape(1, ROWS),
        sequence.reshape(1, ROWS),
    )
    return out.reshape(ROWS, 1, HEADS * HEAD)


def solution(mesh):
    return jax.shard_map(
        body,
        mesh=mesh,
        in_specs=(
            P(("group", "ctx"), "tp"),
            P(("group", "ctx"), "tp", None),
            P(("group", "ctx"), "tp", None),
            P(("group", "ctx")),
            P("tp", None),
            P(None, None, None, "tp", None),
            P("ctx", None, "tp", None),
            P("ctx"),
            P("ctx", None),
            P("ctx"),
        ),
        out_specs=P(("group", "ctx"), "tp", None),
        check_vma=False,
    )
```

time: 258 us -> 78.9 us (0.31)
  the two profiles are of different devices: /device:TPU:2 before, /device:TPU:1 now
where the time goes in v1:
time: 78.9 us; the launch traced here: 78.8 us
  Pallas kernels  77.1 us (98%)
  local copies, waits for them, and re-layouts  1.67 us (2%)
    pallas_call x1, Pallas kernels, body(): pl.pallas_call(kernel, out_shape=jax.ShapeDtypeStruct((ROWS, HEADS * HEAD...  77.1 us
    unnamed x1, local copies, waits for them, and re-layouts  1.67 us

profile of v1, /device:TPU:1, one launch (start us, length us, event | category | flops | bytes accessed | tf_op | source)
XLA Modules:
  0.0 78.8 jit_solution(8143151477582490946)
XLA Ops:
  0.0 77.1 %attention.1 = bf16[128,1024]{1,0:T(8,128)(2,1)} custom-call(bf16[128,1024]{1,0:T(8,128)(2,1)} %hid_ref.1, bf16[128,1024]{1,0:T(8,128)(2,1)} %bitcast.10, bf16[128,256]{1,0:T(8,128)(2,1)} %bitcast.12, s32[1,128]{1,0:T(1,128)} %bitcast.13, bf16[1024,512]{1,0:T(8,128)(2,1)} %down_ref.1, bf16[512,128]{1,0:T(8,128)(2,1)} %bitcast.11, ...), custom_call_target="tpu_custom_call" | custom-call | tf_op jit(solution)/shard_map/attention/pallas_call | solution.py:344
  77.1 1.7 %copy.12 = bf16[128,1,1024]{2,0,1:T(8,128)(2,1)} copy(bf16[128,1,1024]{2,0,1:T(8,128)(2,1)} %bitcast.9) | data formatting | bytes 524288

commit v2 on v1

v2 whole, which is shorter than its diff:
```python
import math

import jax
import jax.numpy as jnp
from jax import lax
from jax.experimental import pallas as pl
from jax.experimental.pallas import tpu as pltpu
from jax.sharding import PartitionSpec as P

MESH = pl.DeviceIdType.MESH
ROWS = 128
HEADS = 8
HEAD = 128
RANK2 = 128
ADAPTERS = 4
SEQ_DEV = 32
CACHE = 128
IDROWS = 8
NZ = 16
NTP = 8
QROWS = ROWS * HEADS
GROUPS = 8
NEG = -1e30
SCALE = math.log2(math.e) / math.sqrt(HEAD)

ORDER = [0, 1, 15, 3, 13, 2, 14, 4, 12, 6, 10, 5, 11, 7, 9, 8]
PLACE = {slot: i for i, slot in enumerate(ORDER)}
CHUNK = 4
CHUNKS = NZ // CHUNK
KEYS = CHUNK * 2 * ROWS
PAGES = CHUNK * 2 * 8
OWN_SENDS = [(0, 3, 3), (0, -3, 13), (0, 1, 1), (0, -1, 15)]
FORWARDS = {
    3: [(3, 3, 6), (3, 1, 4)],
    13: [(13, -3, 10), (13, -1, 12)],
    1: [(1, 1, 2)],
    15: [(15, -1, 14)],
    4: [(4, 1, 5)],
    12: [(12, -1, 11)],
    6: [(6, 2, 8), (6, 1, 7)],
    10: [(10, -1, 9)],
}
RELAYS = [send for sends in FORWARDS.values() for send in sends]
ARRIVALS = [
    (3, 0), (13, 0), (1, 0), (15, 0), (0, 1), (2, 0), (14, 0), (4, 0), (12, 0), (3, 1), (13, 1),
    (1, 1), (15, 1), (6, 0), (10, 0), (2, 1), (14, 1), (4, 1), (12, 1), (5, 0), (11, 0), (6, 1),
    (10, 1), (7, 0), (9, 0), (8, 0), (5, 1), (11, 1), (7, 1), (9, 1), (8, 1),
]
PARTIAL_ORDER = (3, 5, 4, 7, 1, 6, 2)


def kernel(
    hid_ref, q_ref, base_ref, idx_ref, down_ref, up_ref, cache_ref, len_ref, rd_ref, rs_ref,
    out_ref,
    hid, qin, base, idx, down, up, cache, lens, rd, rs,
    part, landed, kv, ids, fresh, choose, handed, q, top, acc, tot, wide,
    load_sem, tp_send, tp_recv, kv_send, kv_recv, core_send, id_send, id_recv,
):
    group = lax.axis_index("group")
    ctx = lax.axis_index("ctx")
    tp = lax.axis_index("tp")
    z = ctx // 2
    x_lo = ctx % 2

    def at(step, other, core):
        side = 1 - x_lo if other else x_lo
        return {"group": core, "ctx": lax.rem(z + step + NZ, NZ) * 2 + side}

    barrier = pltpu.get_barrier_semaphore()

    def greet(peers):
        for peer in peers:
            pl.semaphore_signal(barrier, inc=1, device_id=peer, device_id_type=MESH)

    tp_peers = [{"tp": lax.rem(tp + d, NTP)} for d in range(1, NTP)]
    greet(tp_peers)

    @pl.when(group == 0)
    def _():
        greet([at(0, False, 1)])

    @pl.when(group == 1)
    def _():
        greet([at(step, False, 0) for step in (3, -3, 1, -1, 0)] + [at(0, True, 0)])
        greet([at(step, False, 1) for step in (3, -3, 2, -2, 1, -1)] + [at(0, True, 1)])

    loads = [
        pltpu.make_async_copy(src, dst, load_sem.at[i])
        for i, (src, dst) in enumerate(
            [(hid_ref, hid), (down_ref, down), (idx_ref, idx), (up_ref, up), (base_ref, base),
             (rd_ref, rd), (rs_ref, rs), (q_ref, qin), (len_ref, lens), (cache_ref, cache)]
        )
    ]
    for load in loads[:9]:
        load.start()

    @pl.when(group == 1)
    def _():
        loads[9].start()

    for load in loads[:3]:
        load.wait()

    eye = lax.broadcasted_iota(jnp.int32, (ROWS, ROWS), 0) == lax.broadcasted_iota(
        jnp.int32, (ROWS, ROWS), 1
    )
    adapter = jnp.sum(
        jnp.where(eye, jnp.broadcast_to(idx[...].astype(jnp.float32), (ROWS, ROWS)), 0.0),
        axis=1,
        keepdims=True,
    )
    shrunk = jnp.dot(hid[...], down[...], preferred_element_type=jnp.float32)
    picked = jnp.zeros((ROWS, RANK2), jnp.float32)
    for a in range(ADAPTERS):
        picked = jnp.where(adapter == float(a), shrunk[:, a * RANK2 : (a + 1) * RANK2], picked)
    part[...] = picked

    @pl.when(group == 0)
    def _():
        pl.semaphore_wait(barrier, 13)

    @pl.when(group == 1)
    def _():
        pl.semaphore_wait(barrier, 15)

    tp_copies = [
        pltpu.make_async_remote_copy(
            src_ref=part, dst_ref=landed.at[d],
            send_sem=tp_send.at[d], recv_sem=tp_recv.at[d],
            device_id=tp_peers[d - 1], device_id_type=MESH,
        )
        for d in range(1, NTP)
    ]

    def id_copy(source, step, dest, side):
        i = 2 * dest + side
        return pltpu.make_async_remote_copy(
            src_ref=ids.at[source, 0], dst_ref=ids.at[dest, side],
            send_sem=id_send.at[i], recv_sem=id_recv.at[i],
            device_id=at(step, side == 1, 1), device_id_type=MESH,
        )

    @pl.when(group == 0)
    def _():
        for d in PARTIAL_ORDER:
            tp_copies[d - 1].start()

    for load in loads[3:9]:
        load.wait()

    @pl.when(group == 1)
    def _():
        ids[0, 0] = jnp.concatenate(
            [rd[...], rs[...], jnp.zeros((IDROWS - 2, ROWS), jnp.int32)], axis=0
        )
        for send in OWN_SENDS:
            id_copy(*send, 0).start()
        id_copy(0, 0, 0, 1).start()

    for g in range(GROUPS):
        for j in range(HEADS):
            q[g * 128 + j * 16 : g * 128 + (j + 1) * 16, :] = qin[
                g * 16 : (g + 1) * 16, j * HEAD : (j + 1) * HEAD
            ]
    is_key = (lax.broadcasted_iota(jnp.int32, (ADAPTERS * RANK2, HEAD), 0) // 64) % 2 == 0
    up_f = up[...].astype(jnp.float32)
    wide[:, :HEAD] = jnp.where(is_key, up_f, 0.0).astype(jnp.bfloat16)
    wide[:, HEAD:] = jnp.where(is_key, 0.0, up_f).astype(jnp.bfloat16)

    def scores_of(queries, keys):
        return lax.dot_general(
            queries, keys, (((1,), (1,)), ((), ())), preferred_element_type=jnp.float32
        )

    def weighted(weights, values):
        ones = jnp.ones(values.shape, jnp.bfloat16)
        return jnp.dot(
            weights.astype(jnp.bfloat16),
            jnp.concatenate([values, ones], axis=1),
            preferred_element_type=jnp.float32,
        )

    def first_keys(rows, scores, values):
        peak = jnp.max(scores, axis=1, keepdims=True)
        both = weighted(jnp.exp2((scores - peak) * SCALE), values)
        top[rows, :] = jnp.broadcast_to(peak, (peak.shape[0], HEAD))
        acc[rows, :] = both[:, :HEAD]
        tot[rows, :] = both[:, HEAD:]

    def more_keys(rows, scores, values):
        before = top[rows, :]
        after = jnp.maximum(before, jnp.max(scores, axis=1, keepdims=True))
        rescale = jnp.exp2((before - after) * SCALE)
        both = weighted(jnp.exp2((scores - after[:, :1]) * SCALE), values)
        top[rows, :] = after
        acc[rows, :] = acc[rows, :] * rescale + both[:, :HEAD]
        tot[rows, :] = tot[rows, :] * rescale + both[:, HEAD:]

    row16 = lax.broadcasted_iota(jnp.int32, (128, 1), 0) % 16

    @pl.when(group == 1)
    def _():
        loads[9].wait()
        column = lax.broadcasted_iota(jnp.int32, (1, CACHE), 1)
        for g in range(GROUPS):
            rows = slice(g * 128, (g + 1) * 128)
            block = cache[4 * g : 4 * g + 4].reshape(4 * CACHE, 2 * HEAD)
            scores = scores_of(q[rows, :], block[:, :HEAD])
            own = row16 // 4
            pieces = []
            for n in range(4):
                ok = jnp.logical_and(own == n, column < lens[4 * g + n])
                pieces.append(jnp.where(ok, scores[:, n * CACHE : (n + 1) * CACHE], NEG))
            first_keys(rows, jnp.concatenate(pieces, axis=1), block[:, HEAD:])

        for d in PARTIAL_ORDER:
            tp_copies[d - 1].start()
        for slot, side in ARRIVALS:
            if side == 0:
                id_copy(0, 1, slot, 0).wait_recv()
                for send in FORWARDS.get(slot, []):
                    id_copy(*send, 0).start()
                id_copy(slot, 0, slot, 1).start()
            else:
                id_copy(slot, 0, slot, 1).wait_recv()
        page = lax.broadcasted_iota(jnp.int32, (PAGES, KEYS), 0)
        key = lax.broadcasted_iota(jnp.int32, (PAGES, KEYS), 1)
        same = jnp.logical_and(page // 8 == key // ROWS, page % 8 == key % 8)
        for c in range(CHUNKS):
            slots = ORDER[c * CHUNK : (c + 1) * CHUNK]
            device = jnp.concatenate([ids[s, d, :1] for s in slots for d in (0, 1)], axis=1)
            mine = jnp.logical_and(same, device == ctx)
            choose[c] = jnp.where(mine, 1.0, 0.0).astype(jnp.bfloat16)

    def own_rows():
        for copy in tp_copies:
            copy.wait_recv()
        total = picked
        for d in range(1, NTP):
            total = total + landed[d]
        spread = jnp.concatenate(
            [
                jnp.where(adapter == float(a), total, 0.0).astype(jnp.bfloat16)
                for a in range(ADAPTERS)
            ],
            axis=1,
        )
        delta = jnp.dot(spread, wide[...], preferred_element_type=jnp.float32)
        return (base[...].astype(jnp.float32) + delta).astype(jnp.bfloat16)

    def kv_copy(source, step, dest, side):
        i = 2 * PLACE[dest] + side
        return pltpu.make_async_remote_copy(
            src_ref=kv.at[PLACE[source], 0], dst_ref=kv.at[PLACE[dest], side],
            send_sem=kv_send.at[i], recv_sem=kv_recv.at[i],
            device_id=at(step, side == 1, 1), device_id_type=MESH,
        )

    def core_copy(slot, side):
        i = 2 * PLACE[slot] + side
        return pltpu.make_async_remote_copy(
            src_ref=kv.at[PLACE[slot], side], dst_ref=kv.at[PLACE[slot], side],
            send_sem=core_send.at[i], recv_sem=kv_recv.at[i],
            device_id={"group": 1 - group}, device_id_type=MESH,
        )

    def chunk_of(c):
        block = kv[c * CHUNK : (c + 1) * CHUNK].reshape(KEYS, 2 * HEAD)
        return block[:, :HEAD], block[:, HEAD:]

    @pl.when(group == 0)
    def _():
        kv[0, 0] = own_rows()
        for send in OWN_SENDS:
            kv_copy(*send, 0).start()
        kv_copy(0, 0, 0, 1).start()
        core_copy(0, 0).start()
        for c in range(CHUNKS):
            slots = ORDER[c * CHUNK : (c + 1) * CHUNK]
            for slot in slots:
                for side in (0, 1):
                    if (slot, side) != (0, 0):
                        core_copy(slot, side).wait_recv()
            limit = [jnp.where(z >= slot, 0.0, NEG) for slot in slots for _ in (0, 1)]
            if c == 0:
                limit[1] = jnp.where(x_lo == 1, 0.0, NEG)

            def chunk(c=c, slots=slots, limit=limit):
                keys, values = chunk_of(c)
                bias = jnp.concatenate(
                    [jnp.full((1, ROWS), value, jnp.float32) for value in limit], axis=1
                )
                for g in range(GROUPS):
                    rows = slice(g * 128, (g + 1) * 128)
                    scores = scores_of(q[rows, :], keys) + bias
                    if c == 0:
                        column = lax.broadcasted_iota(jnp.int32, (1, ROWS), 1)
                        diagonal = jnp.where(column <= g * 16 + row16, scores[:, :ROWS], NEG)
                        scores = jnp.concatenate([diagonal, scores[:, ROWS:]], axis=1)
                        first_keys(rows, scores, values)
                    else:
                        more_keys(rows, scores, values)

            if c == 0:
                chunk()
            else:
                pl.when(z >= min(slots))(chunk)

    @pl.when(group == 1)
    def _():
        seen = set()
        core_copy(0, 0).wait_recv()
        seen.add((0, 0))
        ready = 0
        for slot, side in ARRIVALS:
            if side == 0:
                kv_copy(0, 1, slot, 0).wait_recv()
                for send in FORWARDS.get(slot, []):
                    kv_copy(*send, 0).start()
                kv_copy(slot, 0, slot, 1).start()
            else:
                kv_copy(slot, 0, slot, 1).wait_recv()
            core_copy(slot, side).start()
            seen.add((slot, side))
            if (slot, side) == (12, 1):
                fresh[...] = own_rows()
            slots = ORDER[ready * CHUNK : (ready + 1) * CHUNK]
            if all((s, d) in seen for s in slots for d in (0, 1)):
                block = kv[ready * CHUNK : (ready + 1) * CHUNK].reshape(KEYS, 2 * HEAD)
                handed[ready * PAGES : (ready + 1) * PAGES, :] = jnp.dot(
                    choose[ready], block, preferred_element_type=jnp.float32
                ).astype(jnp.bfloat16)
                ready += 1
        assert ready == CHUNKS
        codes = []
        for c in range(CHUNKS):
            slots = ORDER[c * CHUNK : (c + 1) * CHUNK]
            sequence = jnp.concatenate([ids[s, d, 1:2] for s in slots for d in (0, 1)], axis=1)
            sequence = jnp.broadcast_to(sequence.astype(jnp.float32) + 1.0, (16, KEYS))
            codes.append(scores_of(sequence.astype(jnp.bfloat16), choose[c])[:1])
        code = jnp.concatenate(codes, axis=1) - 1.0
        both = jnp.concatenate([handed[...], fresh[...]], axis=0)
        column = lax.broadcasted_iota(jnp.int32, (1, ROWS), 1)
        for g in range(GROUPS):
            rows = slice(g * 128, (g + 1) * 128)
            token = g * 16 + row16
            scores = scores_of(q[rows, :], both[:, :HEAD])
            step_ok = jnp.logical_and(column // 4 == token // 4, column <= token)
            handed_ok = code == (token // 4).astype(jnp.float32)
            scores = jnp.concatenate(
                [
                    jnp.where(handed_ok, scores[:, : CHUNKS * PAGES], NEG),
                    jnp.where(step_ok, scores[:, CHUNKS * PAGES :], NEG),
                ],
                axis=1,
            )
            more_keys(rows, scores, both[:, HEAD:])

    for g in range(GROUPS):
        rows = slice(g * 128, (g + 1) * 128)
        result = (acc[rows, :] / tot[rows, :]).astype(jnp.bfloat16)
        for j in range(HEADS):
            out_ref[g * 16 : (g + 1) * 16, j * HEAD : (j + 1) * HEAD] = result[
                j * 16 : (j + 1) * 16
            ]

    for copy in tp_copies:
        copy.wait_send()

    @pl.when(group == 0)
    def _():
        for send in OWN_SENDS:
            kv_copy(*send, 0).wait_send()
        kv_copy(0, 0, 0, 1).wait_send()
        core_copy(0, 0).wait_send()

    @pl.when(group == 1)
    def _():
        for send in OWN_SENDS:
            id_copy(*send, 0).wait_send()
        id_copy(0, 0, 0, 1).wait_send()
        for send in RELAYS:
            id_copy(*send, 0).wait_send()
            kv_copy(*send, 0).wait_send()
        for slot, side in ARRIVALS:
            core_copy(slot, side).wait_send()
            if side == 0:
                id_copy(slot, 0, slot, 1).wait_send()
                kv_copy(slot, 0, slot, 1).wait_send()


def body(hidden, queries, base, adapter, down, up, cache, lengths, device, sequence):
    vmem = pltpu.VMEM
    dma = pltpu.SemaphoreType.DMA
    bf16, f32, i32 = jnp.bfloat16, jnp.float32, jnp.int32
    out = pl.pallas_call(
        kernel,
        out_shape=jax.ShapeDtypeStruct((ROWS, HEADS * HEAD), bf16),
        in_specs=[pl.BlockSpec(memory_space=pl.ANY)] * 10,
        out_specs=pl.BlockSpec(memory_space=vmem),
        scratch_shapes=[
            vmem((ROWS, 1024), bf16),
            vmem((ROWS, HEADS * HEAD), bf16),
            vmem((ROWS, 2 * HEAD), bf16),
            vmem((1, ROWS), i32),
            vmem((1024, ADAPTERS * RANK2), bf16),
            vmem((ADAPTERS * RANK2, HEAD), bf16),
            vmem((SEQ_DEV, CACHE, 2 * HEAD), bf16),
            pltpu.SMEM((SEQ_DEV,), i32),
            vmem((1, ROWS), i32),
            vmem((1, ROWS), i32),
            vmem((ROWS, RANK2), f32),
            vmem((NTP, ROWS, RANK2), f32),
            vmem((NZ, 2, ROWS, 2 * HEAD), bf16),
            vmem((NZ, 2, IDROWS, ROWS), i32),
            vmem((ROWS, 2 * HEAD), bf16),
            vmem((CHUNKS, PAGES, KEYS), bf16),
            vmem((CHUNKS * PAGES, 2 * HEAD), bf16),
            vmem((QROWS, HEAD), bf16),
            vmem((QROWS, HEAD), f32),
            vmem((QROWS, HEAD), f32),
            vmem((QROWS, HEAD), f32),
            vmem((ADAPTERS * RANK2, 2 * HEAD), bf16),
            dma((10,)), dma((NTP,)), dma((NTP,)), dma((2 * NZ,)), dma((2 * NZ,)),
            dma((2 * NZ,)), dma((2 * NZ,)), dma((2 * NZ,)),
        ],
        compiler_params=pltpu.CompilerParams(
            collective_id=0, has_side_effects=True, vmem_limit_bytes=60 << 20
        ),
        name="attention",
    )(
        hidden,
        queries.reshape(ROWS, HEADS * HEAD),
        base.reshape(ROWS, 2 * HEAD),
        adapter.reshape(1, ROWS),
        down,
        up.reshape(ADAPTERS * RANK2, HEAD),
        cache.reshape(SEQ_DEV, CACHE, 2 * HEAD),
        lengths,
        device.reshape(1, ROWS),
        sequence.reshape(1, ROWS),
    )
    return out.reshape(ROWS, 1, HEADS * HEAD)


def solution(mesh):
    return jax.shard_map(
        body,
        mesh=mesh,
        in_specs=(
            P(("group", "ctx"), "tp"),
            P(("group", "ctx"), "tp", None),
            P(("group", "ctx"), "tp", None),
            P(("group", "ctx")),
            P("tp", None),
            P(None, None, None, "tp", None),
            P("ctx", None, "tp", None),
            P("ctx"),
            P("ctx", None),
            P("ctx"),
        ),
        out_specs=P(("group", "ctx"), "tp", None),
        check_vma=False,
    )
```

time: 78.9 us -> 52 us (0.66)
  Pallas kernels: 77.1 us -> 50.1 us
    pallas_call x1, Pallas kernels: 77.1 us -> 50.1 us  [body(): pl.pallas_call(kernel, out_shape=jax.ShapeDtypeStruct((ROWS, HEADS * HEAD...]
where the time goes in v2:
time: 52 us; the launch traced here: 51.8 us
  Pallas kernels  50.1 us (96%)
  local copies, waits for them, and re-layouts  1.67 us (3%)
    pallas_call x1, Pallas kernels, body(): pl.pallas_call(kernel, out_shape=jax.ShapeDtypeStruct((ROWS, HEADS * HEAD...  50.1 us
    unnamed x1, local copies, waits for them, and re-layouts  1.67 us

profile of v2, /device:TPU:1, one launch (start us, length us, event | category | flops | bytes accessed | tf_op | source)
XLA Modules:
  0.0 51.8 jit_solution(5180364110385565312)
XLA Ops:
  0.0 50.1 %attention.1 = bf16[128,1024]{1,0:T(8,128)(2,1)} custom-call(bf16[128,1024]{1,0:T(8,128)(2,1)} %hid_ref.1, bf16[128,1024]{1,0:T(8,128)(2,1)} %bitcast.10, bf16[128,256]{1,0:T(8,128)(2,1)} %bitcast.12, s32[1,128]{1,0:T(1,128)} %bitcast.13, bf16[1024,512]{1,0:T(8,128)(2,1)} %down_ref.1, bf16[512,128]{1,0:T(8,128)(2,1)} %bitcast.11, ...), custom_call_target="tpu_custom_call" | custom-call | tf_op jit(solution)/shard_map/attention/pallas_call | solution.py:396
  50.1 1.7 %copy.12 = bf16[128,1,1024]{2,0,1:T(8,128)(2,1)} copy(bf16[128,1,1024]{2,0,1:T(8,128)(2,1)} %bitcast.9) | data formatting | bytes 524288

commit v3 on v2

--- a/solution.py
+++ b/solution.py
@@ -46,6 +46,7 @@
     (1, 1), (15, 1), (6, 0), (10, 0), (2, 1), (14, 1), (4, 1), (12, 1), (5, 0), (11, 0), (6, 1),
     (10, 1), (7, 0), (9, 0), (8, 0), (5, 1), (11, 1), (7, 1), (9, 1), (8, 1),
 ]
+BOTH = (7, 8, 9)
 PARTIAL_ORDER = (3, 5, 4, 7, 1, 6, 2)
 
 
@@ -53,8 +54,9 @@
     hid_ref, q_ref, base_ref, idx_ref, down_ref, up_ref, cache_ref, len_ref, rd_ref, rs_ref,
     out_ref,
     hid, qin, base, idx, down, up, cache, lens, rd, rs,
-    part, landed, kv, ids, fresh, choose, handed, q, top, acc, tot, wide,
+    part, landed, whole, kv, ids, fresh, choose, handed, q, top, acc, tot, wide,
     load_sem, tp_send, tp_recv, kv_send, kv_recv, core_send, id_send, id_recv,
+    share_send, share_recv,
 ):
     group = lax.axis_index("group")
     ctx = lax.axis_index("ctx")
@@ -83,6 +85,7 @@
     def _():
         greet([at(step, False, 0) for step in (3, -3, 1, -1, 0)] + [at(0, True, 0)])
         greet([at(step, False, 1) for step in (3, -3, 2, -2, 1, -1)] + [at(0, True, 1)])
+        greet([at(step, True, 1) for step in (-2, -1, 1)])
 
     loads = [
         pltpu.make_async_copy(src, dst, load_sem.at[i])
@@ -121,12 +124,32 @@
 
     @pl.when(group == 1)
     def _():
-        pl.semaphore_wait(barrier, 15)
+        pl.semaphore_wait(barrier, 18)
 
     tp_copies = [
         pltpu.make_async_remote_copy(
             src_ref=part, dst_ref=landed.at[d],
             send_sem=tp_send.at[d], recv_sem=tp_recv.at[d],
+            device_id=tp_peers[d - 1], device_id_type=MESH,
+        )
+        for d in range(1, NTP)
+    ]
+
+    def piece(index):
+        return pl.ds(pl.multiple_of(index * 16, 16), 16)
+
+    piece_copies = [
+        pltpu.make_async_remote_copy(
+            src_ref=part.at[piece(lax.rem(tp + d, NTP))], dst_ref=landed.at[d, :16],
+            send_sem=tp_send.at[d], recv_sem=tp_recv.at[d],
+            device_id=tp_peers[d - 1], device_id_type=MESH,
+        )
+        for d in range(1, NTP)
+    ]
+    share_copies = [
+        pltpu.make_async_remote_copy(
+            src_ref=whole.at[piece(tp)], dst_ref=whole.at[piece(tp)],
+            send_sem=share_send.at[d], recv_sem=share_recv.at[d],
             device_id=tp_peers[d - 1], device_id_type=MESH,
         )
         for d in range(1, NTP)
@@ -153,6 +176,8 @@
         ids[0, 0] = jnp.concatenate(
             [rd[...], rs[...], jnp.zeros((IDROWS - 2, ROWS), jnp.int32)], axis=0
         )
+        for d in PARTIAL_ORDER:
+            piece_copies[d - 1].start()
         for send in OWN_SENDS:
             id_copy(*send, 0).start()
         id_copy(0, 0, 0, 1).start()
@@ -213,8 +238,13 @@
                 pieces.append(jnp.where(ok, scores[:, n * CACHE : (n + 1) * CACHE], NEG))
             first_keys(rows, jnp.concatenate(pieces, axis=1), block[:, HEAD:])
 
+        summed = part[piece(tp), :]
+        for d in range(1, NTP):
+            piece_copies[d - 1].wait_recv()
+            summed = summed + landed[d, :16]
+        whole[piece(tp), :] = summed.astype(jnp.bfloat16)
         for d in PARTIAL_ORDER:
-            tp_copies[d - 1].start()
+            share_copies[d - 1].start()
         for slot, side in ARRIVALS:
             if side == 0:
                 id_copy(0, 1, slot, 0).wait_recv()
@@ -232,12 +262,7 @@
             mine = jnp.logical_and(same, device == ctx)
             choose[c] = jnp.where(mine, 1.0, 0.0).astype(jnp.bfloat16)
 
-    def own_rows():
-        for copy in tp_copies:
-            copy.wait_recv()
-        total = picked
-        for d in range(1, NTP):
-            total = total + landed[d]
+    def own_rows(total):
         spread = jnp.concatenate(
             [
                 jnp.where(adapter == float(a), total, 0.0).astype(jnp.bfloat16)
@@ -270,7 +295,11 @@
 
     @pl.when(group == 0)
     def _():
-        kv[0, 0] = own_rows()
+        total = picked
+        for d in range(1, NTP):
+            tp_copies[d - 1].wait_recv()
+            total = total + landed[d]
+        kv[0, 0] = own_rows(total)
         for send in OWN_SENDS:
             kv_copy(*send, 0).start()
         kv_copy(0, 0, 0, 1).start()
@@ -317,13 +346,18 @@
                 kv_copy(0, 1, slot, 0).wait_recv()
                 for send in FORWARDS.get(slot, []):
                     kv_copy(*send, 0).start()
-                kv_copy(slot, 0, slot, 1).start()
+                    if send[2] in BOTH:
+                        kv_copy(*send, 1).start()
+                if slot not in BOTH:
+                    kv_copy(slot, 0, slot, 1).start()
             else:
                 kv_copy(slot, 0, slot, 1).wait_recv()
             core_copy(slot, side).start()
             seen.add((slot, side))
             if (slot, side) == (12, 1):
-                fresh[...] = own_rows()
+                for copy in share_copies:
+                    copy.wait_recv()
+                fresh[...] = own_rows(whole[...].astype(jnp.float32))
             slots = ORDER[ready * CHUNK : (ready + 1) * CHUNK]
             if all((s, d) in seen for s in slots for d in (0, 1)):
                 block = kv[ready * CHUNK : (ready + 1) * CHUNK].reshape(KEYS, 2 * HEAD)
@@ -364,11 +398,10 @@
                 j * 16 : (j + 1) * 16
             ]
 
-    for copy in tp_copies:
-        copy.wait_send()
-
     @pl.when(group == 0)
     def _():
+        for copy in tp_copies:
+            copy.wait_send()
         for send in OWN_SENDS:
             kv_copy(*send, 0).wait_send()
         kv_copy(0, 0, 0, 1).wait_send()
@@ -376,17 +409,22 @@
 
     @pl.when(group == 1)
     def _():
+        for copy in piece_copies + share_copies:
+            copy.wait_send()
         for send in OWN_SENDS:
             id_copy(*send, 0).wait_send()
         id_copy(0, 0, 0, 1).wait_send()
         for send in RELAYS:
             id_copy(*send, 0).wait_send()
             kv_copy(*send, 0).wait_send()
+            if send[2] in BOTH:
+                kv_copy(*send, 1).wait_send()
         for slot, side in ARRIVALS:
             core_copy(slot, side).wait_send()
             if side == 0:
                 id_copy(slot, 0, slot, 1).wait_send()
-                kv_copy(slot, 0, slot, 1).wait_send()
+                if slot not in BOTH:
+                    kv_copy(slot, 0, slot, 1).wait_send()
 
 
 def body(hidden, queries, base, adapter, down, up, cache, lengths, device, sequence):
@@ -411,6 +449,7 @@
             vmem((1, ROWS), i32),
             vmem((ROWS, RANK2), f32),
             vmem((NTP, ROWS, RANK2), f32),
+            vmem((ROWS, RANK2), bf16),
             vmem((NZ, 2, ROWS, 2 * HEAD), bf16),
             vmem((NZ, 2, IDROWS, ROWS), i32),
             vmem((ROWS, 2 * HEAD), bf16),
@@ -422,7 +461,7 @@
             vmem((QROWS, HEAD), f32),
             vmem((ADAPTERS * RANK2, 2 * HEAD), bf16),
             dma((10,)), dma((NTP,)), dma((NTP,)), dma((2 * NZ,)), dma((2 * NZ,)),
-            dma((2 * NZ,)), dma((2 * NZ,)), dma((2 * NZ,)),
+            dma((2 * NZ,)), dma((2 * NZ,)), dma((2 * NZ,)), dma((NTP,)), dma((NTP,)),
         ],
         compiler_params=pltpu.CompilerParams(
             collective_id=0, has_side_effects=True, vmem_limit_bytes=60 << 20

time: 52 us -> 48.6 us (0.935)
  Pallas kernels: 50.1 us -> 46.7 us
    pallas_call x1, Pallas kernels: 50.1 us -> 46.7 us  [body(): pl.pallas_call(kernel, out_shape=jax.ShapeDtypeStruct((ROWS, HEADS * HEAD...]
where the time goes in v3:
time: 48.6 us; the launch traced here: 48.4 us
  Pallas kernels  46.7 us (96%)
  local copies, waits for them, and re-layouts  1.67 us (3%)
    pallas_call x1, Pallas kernels, body(): pl.pallas_call(kernel, out_shape=jax.ShapeDtypeStruct((ROWS, HEADS * HEAD...  46.7 us
    unnamed x1, local copies, waits for them, and re-layouts  1.67 us

profile of v3, /device:TPU:1, one launch (start us, length us, event | category | flops | bytes accessed | tf_op | source)
XLA Modules:
  0.0 48.4 jit_solution(12441397660579181623)
XLA Ops:
  0.0 46.7 %attention.1 = bf16[128,1024]{1,0:T(8,128)(2,1)} custom-call(bf16[128,1024]{1,0:T(8,128)(2,1)} %hid_ref.1, bf16[128,1024]{1,0:T(8,128)(2,1)} %bitcast.10, bf16[128,256]{1,0:T(8,128)(2,1)} %bitcast.12, s32[1,128]{1,0:T(1,128)} %bitcast.13, bf16[1024,512]{1,0:T(8,128)(2,1)} %down_ref.1, bf16[512,128]{1,0:T(8,128)(2,1)} %bitcast.11, ...), custom_call_target="tpu_custom_call" | custom-call | tf_op jit(solution)/shard_map/attention/pallas_call | solution.py:434
  46.7 1.7 %copy.12 = bf16[128,1,1024]{2,0,1:T(8,128)(2,1)} copy(bf16[128,1,1024]{2,0,1:T(8,128)(2,1)} %bitcast.9) | data formatting | bytes 524288

commit v4 on v3

--- a/solution.py
+++ b/solution.py
@@ -47,6 +47,7 @@
     (10, 1), (7, 0), (9, 0), (8, 0), (5, 1), (11, 1), (7, 1), (9, 1), (8, 1),
 ]
 BOTH = (7, 8, 9)
+LAST = 256
 PARTIAL_ORDER = (3, 5, 4, 7, 1, 6, 2)
 
 
@@ -54,7 +55,7 @@
     hid_ref, q_ref, base_ref, idx_ref, down_ref, up_ref, cache_ref, len_ref, rd_ref, rs_ref,
     out_ref,
     hid, qin, base, idx, down, up, cache, lens, rd, rs,
-    part, landed, whole, kv, ids, fresh, choose, handed, q, top, acc, tot, wide,
+    part, landed, whole, kv, ids, fresh, choose, code_row, handed, q, top, acc, tot, wide,
     load_sem, tp_send, tp_recv, kv_send, kv_recv, core_send, id_send, id_recv,
     share_send, share_recv,
 ):
@@ -221,7 +222,25 @@
         acc[rows, :] = acc[rows, :] * rescale + both[:, :HEAD]
         tot[rows, :] = tot[rows, :] * rescale + both[:, HEAD:]
 
+    def emit(group_row, result):
+        for g in range(result.shape[0] // 128):
+            first = (group_row + g) * 16
+            for j in range(HEADS):
+                start = g * 128 + j * 16
+                out_ref[first : first + 16, j * HEAD : (j + 1) * HEAD] = result[start : start + 16]
+
     row16 = lax.broadcasted_iota(jnp.int32, (128, 1), 0) % 16
+
+    def own_rows(total):
+        spread = jnp.concatenate(
+            [
+                jnp.where(adapter == float(a), total, 0.0).astype(jnp.bfloat16)
+                for a in range(ADAPTERS)
+            ],
+            axis=1,
+        )
+        delta = jnp.dot(spread, wide[...], preferred_element_type=jnp.float32)
+        return (base[...].astype(jnp.float32) + delta).astype(jnp.bfloat16)
 
     @pl.when(group == 1)
     def _():
@@ -253,25 +272,28 @@
                 id_copy(slot, 0, slot, 1).start()
             else:
                 id_copy(slot, 0, slot, 1).wait_recv()
+            if (slot, side) == (5, 1):
+                for copy in share_copies:
+                    copy.wait_recv()
+                fresh[...] = own_rows(whole[...].astype(jnp.float32))
         page = lax.broadcasted_iota(jnp.int32, (PAGES, KEYS), 0)
         key = lax.broadcasted_iota(jnp.int32, (PAGES, KEYS), 1)
         same = jnp.logical_and(page // 8 == key // ROWS, page % 8 == key % 8)
+        spread8 = lax.broadcasted_iota(
+            jnp.int32, (2 * CHUNK, PAGES), 0
+        ) == lax.broadcasted_iota(jnp.int32, (2 * CHUNK, PAGES), 1) // 8
+        codes = []
         for c in range(CHUNKS):
             slots = ORDER[c * CHUNK : (c + 1) * CHUNK]
             device = jnp.concatenate([ids[s, d, :1] for s in slots for d in (0, 1)], axis=1)
             mine = jnp.logical_and(same, device == ctx)
             choose[c] = jnp.where(mine, 1.0, 0.0).astype(jnp.bfloat16)
-
-    def own_rows(total):
-        spread = jnp.concatenate(
-            [
-                jnp.where(adapter == float(a), total, 0.0).astype(jnp.bfloat16)
-                for a in range(ADAPTERS)
-            ],
-            axis=1,
-        )
-        delta = jnp.dot(spread, wide[...], preferred_element_type=jnp.float32)
-        return (base[...].astype(jnp.float32) + delta).astype(jnp.bfloat16)
+            device = jnp.concatenate([ids[s, d, :1] for s in slots for d in (0, 1)], axis=0)
+            sequence = jnp.concatenate([ids[s, d, 1:2] for s in slots for d in (0, 1)], axis=0)
+            sequence = jnp.where(device == ctx, sequence, -1).astype(jnp.float32)
+            sequence = jnp.max(sequence, axis=1, keepdims=True)
+            codes.append(jnp.sum(jnp.where(spread8, sequence, 0.0), axis=0, keepdims=True))
+        code_row[...] = jnp.broadcast_to(jnp.concatenate(codes, axis=1), code_row.shape)
 
     def kv_copy(source, step, dest, side):
         i = 2 * PLACE[dest] + side
@@ -354,10 +376,6 @@
                 kv_copy(slot, 0, slot, 1).wait_recv()
             core_copy(slot, side).start()
             seen.add((slot, side))
-            if (slot, side) == (12, 1):
-                for copy in share_copies:
-                    copy.wait_recv()
-                fresh[...] = own_rows(whole[...].astype(jnp.float32))
             slots = ORDER[ready * CHUNK : (ready + 1) * CHUNK]
             if all((s, d) in seen for s in slots for d in (0, 1)):
                 block = kv[ready * CHUNK : (ready + 1) * CHUNK].reshape(KEYS, 2 * HEAD)
@@ -366,18 +384,13 @@
                 ).astype(jnp.bfloat16)
                 ready += 1
         assert ready == CHUNKS
-        codes = []
-        for c in range(CHUNKS):
-            slots = ORDER[c * CHUNK : (c + 1) * CHUNK]
-            sequence = jnp.concatenate([ids[s, d, 1:2] for s in slots for d in (0, 1)], axis=1)
-            sequence = jnp.broadcast_to(sequence.astype(jnp.float32) + 1.0, (16, KEYS))
-            codes.append(scores_of(sequence.astype(jnp.bfloat16), choose[c])[:1])
-        code = jnp.concatenate(codes, axis=1) - 1.0
+        code = code_row[:1, :]
         both = jnp.concatenate([handed[...], fresh[...]], axis=0)
         column = lax.broadcasted_iota(jnp.int32, (1, ROWS), 1)
-        for g in range(GROUPS):
-            rows = slice(g * 128, (g + 1) * 128)
-            token = g * 16 + row16
+        row = lax.broadcasted_iota(jnp.int32, (LAST, 1), 0)
+        for i in range(QROWS // LAST):
+            rows = slice(i * LAST, (i + 1) * LAST)
+            token = (i * (LAST // 128) + row // 128) * 16 + row % 16
             scores = scores_of(q[rows, :], both[:, :HEAD])
             step_ok = jnp.logical_and(column // 4 == token // 4, column <= token)
             handed_ok = code == (token // 4).astype(jnp.float32)
@@ -388,15 +401,19 @@
                 ],
                 axis=1,
             )
-            more_keys(rows, scores, both[:, HEAD:])
-
-    for g in range(GROUPS):
-        rows = slice(g * 128, (g + 1) * 128)
-        result = (acc[rows, :] / tot[rows, :]).astype(jnp.bfloat16)
-        for j in range(HEADS):
-            out_ref[g * 16 : (g + 1) * 16, j * HEAD : (j + 1) * HEAD] = result[
-                j * 16 : (j + 1) * 16
-            ]
+            before = top[rows, :]
+            after = jnp.maximum(before, jnp.max(scores, axis=1, keepdims=True))
+            rescale = jnp.exp2((before - after) * SCALE)
+            sums = weighted(jnp.exp2((scores - after[:, :1]) * SCALE), both[:, HEAD:])
+            total = tot[rows, :] * rescale + sums[:, HEAD:]
+            result = (acc[rows, :] * rescale + sums[:, :HEAD]) / total
+            emit(i * (LAST // 128), result.astype(jnp.bfloat16))
+
+    @pl.when(group == 0)
+    def _():
+        for g in range(GROUPS):
+            rows = slice(g * 128, (g + 1) * 128)
+            emit(g, (acc[rows, :] / tot[rows, :]).astype(jnp.bfloat16))
 
     @pl.when(group == 0)
     def _():
@@ -454,6 +471,7 @@
             vmem((NZ, 2, IDROWS, ROWS), i32),
             vmem((ROWS, 2 * HEAD), bf16),
             vmem((CHUNKS, PAGES, KEYS), bf16),
+            vmem((8, CHUNKS * PAGES), f32),
             vmem((CHUNKS * PAGES, 2 * HEAD), bf16),
             vmem((QROWS, HEAD), bf16),
             vmem((QROWS, HEAD), f32),

time: 48.6 us -> 48.1 us (0.990)
  no operation moved by 1% of the time
where the time goes in v4:
time: 48.1 us; the launch traced here: 48 us
  Pallas kernels  46.3 us (96%)
  local copies, waits for them, and re-layouts  1.67 us (3%)
    pallas_call x1, Pallas kernels, body(): pl.pallas_call(kernel, out_shape=jax.ShapeDtypeStruct((ROWS, HEADS * HEAD...  46.3 us
    unnamed x1, local copies, waits for them, and re-layouts  1.67 us

profile of v4, /device:TPU:1, one launch (start us, length us, event | category | flops | bytes accessed | tf_op | source)
XLA Modules:
  0.0 48.0 jit_solution(1379482179253979873)
XLA Ops:
  0.0 46.3 %attention.1 = bf16[128,1024]{1,0:T(8,128)(2,1)} custom-call(bf16[128,1024]{1,0:T(8,128)(2,1)} %hid_ref.1, bf16[128,1024]{1,0:T(8,128)(2,1)} %bitcast.10, bf16[128,256]{1,0:T(8,128)(2,1)} %bitcast.12, s32[1,128]{1,0:T(1,128)} %bitcast.13, bf16[1024,512]{1,0:T(8,128)(2,1)} %down_ref.1, bf16[512,128]{1,0:T(8,128)(2,1)} %bitcast.11, ...), custom_call_target="tpu_custom_call" | custom-call | tf_op jit(solution)/shard_map/attention/pallas_call | solution.py:451
  46.3 1.7 %copy.12 = bf16[128,1,1024]{2,0,1:T(8,128)(2,1)} copy(bf16[128,1,1024]{2,0,1:T(8,128)(2,1)} %bitcast.9) | data formatting | bytes 524288

commit v5 on v4

--- a/solution.py
+++ b/solution.py
@@ -42,8 +42,8 @@
 }
 RELAYS = [send for sends in FORWARDS.values() for send in sends]
 ARRIVALS = [
-    (3, 0), (13, 0), (1, 0), (15, 0), (0, 1), (2, 0), (14, 0), (4, 0), (12, 0), (3, 1), (13, 1),
-    (1, 1), (15, 1), (6, 0), (10, 0), (2, 1), (14, 1), (4, 1), (12, 1), (5, 0), (11, 0), (6, 1),
+    (3, 0), (13, 0), (1, 0), (15, 0), (4, 0), (12, 0), (2, 0), (14, 0), (6, 0), (10, 0), (0, 1),
+    (3, 1), (13, 1), (1, 1), (15, 1), (5, 0), (11, 0), (2, 1), (14, 1), (4, 1), (12, 1), (6, 1),
     (10, 1), (7, 0), (9, 0), (8, 0), (5, 1), (11, 1), (7, 1), (9, 1), (8, 1),
 ]
 BOTH = (7, 8, 9)

time: 48.1 us -> 47.3 us (0.983)
  Pallas kernels: 46.3 us -> 45.4 us
    pallas_call x1, Pallas kernels: 46.3 us -> 45.4 us  [body(): pl.pallas_call(kernel, out_shape=jax.ShapeDtypeStruct((ROWS, HEADS * HEAD...]
where the time goes in v5:
time: 47.3 us; the launch traced here: 47.1 us
  Pallas kernels  45.4 us (96%)
  local copies, waits for them, and re-layouts  1.67 us (4%)
    pallas_call x1, Pallas kernels, body(): pl.pallas_call(kernel, out_shape=jax.ShapeDtypeStruct((ROWS, HEADS * HEAD...  45.4 us
    unnamed x1, local copies, waits for them, and re-layouts  1.67 us

profile of v5, /device:TPU:1, one launch (start us, length us, event | category | flops | bytes accessed | tf_op | source)
XLA Modules:
  0.0 47.1 jit_solution(4299611012162029592)
XLA Ops:
  0.0 45.4 %attention.1 = bf16[128,1024]{1,0:T(8,128)(2,1)} custom-call(bf16[128,1024]{1,0:T(8,128)(2,1)} %hid_ref.1, bf16[128,1024]{1,0:T(8,128)(2,1)} %bitcast.10, bf16[128,256]{1,0:T(8,128)(2,1)} %bitcast.12, s32[1,128]{1,0:T(1,128)} %bitcast.13, bf16[1024,512]{1,0:T(8,128)(2,1)} %down_ref.1, bf16[512,128]{1,0:T(8,128)(2,1)} %bitcast.11, ...), custom_call_target="tpu_custom_call" | custom-call | tf_op jit(solution)/shard_map/attention/pallas_call | solution.py:451
  45.4 1.7 %copy.12 = bf16[128,1,1024]{2,0,1:T(8,128)(2,1)} copy(bf16[128,1,1024]{2,0,1:T(8,128)(2,1)} %bitcast.9) | data formatting | bytes 524288

commit v6 on v5

--- a/solution.py
+++ b/solution.py
@@ -360,7 +360,6 @@
     @pl.when(group == 1)
     def _():
         seen = set()
-        core_copy(0, 0).wait_recv()
         seen.add((0, 0))
         ready = 0
         for slot, side in ARRIVALS:
@@ -376,6 +375,8 @@
                 kv_copy(slot, 0, slot, 1).wait_recv()
             core_copy(slot, side).start()
             seen.add((slot, side))
+            if (slot, side) == (0, 1):
+                core_copy(0, 0).wait_recv()
             slots = ORDER[ready * CHUNK : (ready + 1) * CHUNK]
             if all((s, d) in seen for s in slots for d in (0, 1)):
                 block = kv[ready * CHUNK : (ready + 1) * CHUNK].reshape(KEYS, 2 * HEAD)

time: 47.3 us -> 47.3 us (level)
  no operation moved by 1% of the time
where the time goes in v6:
time: 47.3 us; the launch traced here: 47.1 us
  Pallas kernels  45.4 us (96%)
  local copies, waits for them, and re-layouts  1.67 us (4%)
    pallas_call x1, Pallas kernels, body(): pl.pallas_call(kernel, out_shape=jax.ShapeDtypeStruct((ROWS, HEADS * HEAD...  45.4 us
    unnamed x1, local copies, waits for them, and re-layouts  1.67 us

profile of v6, /device:TPU:1, one launch (start us, length us, event | category | flops | bytes accessed | tf_op | source)
XLA Modules:
  0.0 47.1 jit_solution(6962260576153755604)
XLA Ops:
  0.0 45.4 %attention.1 = bf16[128,1024]{1,0:T(8,128)(2,1)} custom-call(bf16[128,1024]{1,0:T(8,128)(2,1)} %hid_ref.1, bf16[128,1024]{1,0:T(8,128)(2,1)} %bitcast.10, bf16[128,256]{1,0:T(8,128)(2,1)} %bitcast.12, s32[1,128]{1,0:T(1,128)} %bitcast.13, bf16[1024,512]{1,0:T(8,128)(2,1)} %down_ref.1, bf16[512,128]{1,0:T(8,128)(2,1)} %bitcast.11, ...), custom_call_target="tpu_custom_call" | custom-call | tf_op jit(solution)/shard_map/attention/pallas_call | solution.py:452
  45.4 1.7 %copy.12 = bf16[128,1,1024]{2,0,1:T(8,128)(2,1)} copy(bf16[128,1,1024]{2,0,1:T(8,128)(2,1)} %bitcast.9) | data formatting | bytes 524288
